TPU v7x, 32 devices: a whole 2x2x4 slice. The times are simulated.
32 devices in a mesh: side: 2 (over core), grp: 4 (over y, x), blk: 4 (over z).
Axes of the slice: x: 2, y: 2, z: 4, core: 2. Of those that a mesh axis runs over, the one named last changes fastest.
Arguments:
- node_modes: bfloat16 [3, 16384, 256], P(None, ('grp', 'blk'), 'side'), may hold values from -6 to 6
- node_index: int32 [4, 24576], P(None, ('grp', 'blk')), may hold values from 0 to 1023
- interp: float32 [4, 24576], P(None, ('grp', 'blk')), may hold values from 0.1 to 1
- normals: float32 [3, 24576], P(None, ('grp', 'blk')), may hold values from -6 to 6
- counts: int32 [16, 16], P(None, ('grp', 'blk')), may hold values from 0 to 96, as said below
- inverse_diag: bfloat16 [16384, 1024], P(('grp', 'blk'))
- lower_left: bfloat16 [16384, 32], P(('grp', 'blk')), may hold values from -0.375 to 0.375
- lower_right: bfloat16 [16384, 32], P(('grp', 'blk')), may hold values from -0.09375 to 0.09375
- upper_left: bfloat16 [16384, 32], P(('grp', 'blk')), may hold values from -0.375 to 0.375
- upper_right: bfloat16 [16384, 32], P(('grp', 'blk')), may hold values from -0.09375 to 0.09375
- ranks: int32 [16], P(('grp', 'blk')), may hold values from 8 to 32
- areas: float32 [16384], P(('grp', 'blk')), may hold values from 0.00390625 to 0.03125
Outputs:
- potentials: bfloat16 [16384, 256], P(('grp', 'blk'), 'side')
- added_mass: float32 [256, 256], P(('grp', 'blk'), 'side')
Inputs may be any that keep to these rules, and one draw needn't show every extreme that they name: In each column d the counts sum to 1024, and every column holds one count equal to 96.
All inputs are finite; a program needn't handle non-finite values.
Results may differ from a plain program's by a relative error of at most 0.0049.
Values may be sent and summed in bfloat16 or wider, within the bound.
A program may use at most 64 MiB of HBM per device.

v0:
```python
import jax
import jax.numpy as jnp
from jax import lax
from jax.sharding import PartitionSpec as P

HIGH = lax.Precision.HIGHEST


def entering(value, axis, join, neutral, backward):
    count, mine = (lax.axis_size(axis), lax.axis_index(axis))
    pieces = jax.tree.map(lambda part: lax.all_gather(part, axis), value)
    if backward:
        pieces = jax.tree.map(lambda part: part[::-1], pieces)
        mine = count - 1 - mine
    total = jax.tree.map(
        lambda part, zero: jnp.full_like(part, 0) + jnp.asarray(zero, part.dtype), value, neutral
    )

    def turn(position, total):
        longer = join(total, jax.tree.map(lambda part: part[position], pieces))
        return jax.tree.map(lambda new, old: jnp.where(position < mine, new, old), longer, total)

    return lax.fori_loop(0, count - 1, turn, total)


def compose(earlier, later):
    return (
        jnp.dot(later[0], earlier[0], precision=HIGH),
        jnp.dot(later[0], earlier[1], precision=HIGH) + later[1],
    )


def body(
    node_modes,
    node_index,
    interp,
    normals,
    counts,
    inverse_diag,
    lower_left,
    lower_right,
    upper_left,
    upper_right,
    ranks,
    areas,
):
    devices = lax.axis_size(("grp", "blk"))
    width = node_modes.shape[2]
    slot_total = node_index.shape[1]
    capacity = slot_total // devices
    velocity = jnp.zeros((slot_total, width), jnp.float32)
    for corner in range(4):
        picked = jnp.take(node_modes, node_index[corner], axis=1)
        for axis_id in range(3):
            weight_now = interp[corner] * normals[axis_id]
            velocity = velocity + weight_now[:, None] * picked[axis_id].astype(jnp.float32)
    outgoing = velocity.astype(jnp.bfloat16).reshape(devices, capacity, width)
    group_count = lax.axis_size("grp")
    block_count = lax.axis_size("blk")
    sectioned = outgoing.reshape(group_count, block_count, capacity, width)
    arrived = lax.all_to_all(
        lax.all_to_all(sectioned, "grp", split_axis=0, concat_axis=0, tiled=True),
        "blk",
        split_axis=1,
        concat_axis=1,
        tiled=True,
    )
    arrived = arrived.reshape(devices * capacity, width)
    panels = inverse_diag.shape[0]
    column = counts[:, 0]
    cum_ends = jnp.cumsum(column)
    cum_starts = cum_ends - column
    position = jnp.arange(panels, dtype=jnp.int32)
    owner = jnp.sum((cum_ends[None, :] <= position[:, None]).astype(jnp.int32), axis=1)
    owner_hot = owner[:, None] == jnp.arange(devices, dtype=jnp.int32)[None, :]
    owner_start = jnp.sum(jnp.where(owner_hot, cum_starts[None, :], 0), axis=1)
    row_ids = owner * capacity + position - owner_start
    normal_velocity = jnp.take(arrived, row_ids, axis=0)
    rank_width = lower_left.shape[1]
    keep = (jnp.arange(rank_width, dtype=jnp.int32) < ranks[0])[None, :]
    lower_masked = jnp.where(keep, lower_left, jnp.zeros_like(lower_left))
    upper_masked = jnp.where(keep, upper_left, jnp.zeros_like(upper_left)).astype(jnp.float32)
    solved = jnp.dot(inverse_diag, normal_velocity, preferred_element_type=jnp.float32)
    spread = jnp.dot(inverse_diag, lower_masked, preferred_element_type=jnp.float32)
    identity = jnp.eye(rank_width, dtype=jnp.float32)
    zero_state = jnp.zeros((rank_width, width), jnp.float32)
    right_lower = lower_right.astype(jnp.float32)
    forward_map = identity - jnp.dot(right_lower.T, spread, precision=HIGH)
    forward_shift = jnp.dot(right_lower.T, solved, precision=HIGH)
    ignored, incoming = entering(
        (forward_map, forward_shift), ("grp", "blk"), compose, (identity, zero_state), False
    )
    interim = solved - jnp.dot(spread, incoming, precision=HIGH)
    right_upper = upper_right.astype(jnp.float32)
    backward_map = identity - jnp.dot(right_upper.T, upper_masked, precision=HIGH)
    backward_shift = jnp.dot(right_upper.T, interim, precision=HIGH)
    ignored, from_above = entering(
        (backward_map, backward_shift), ("grp", "blk"), compose, (identity, zero_state), True
    )
    potentials = (interim - jnp.dot(upper_masked, from_above, precision=HIGH)).astype(jnp.bfloat16)
    weighted = (areas[:, None] * potentials.astype(jnp.float32)).astype(jnp.bfloat16)
    all_modes = lax.all_gather(normal_velocity, "side", axis=1, tiled=True)
    added_mass = lax.psum_scatter(
        lax.dot_general(
            all_modes, weighted, (((0,), (0,)), ((), ())), preferred_element_type=jnp.float32
        ),
        ("grp", "blk"),
        scatter_dimension=0,
        tiled=True,
    )
    return (potentials, added_mass)


def solution(mesh):
    in_specs = (
        P(None, ("grp", "blk"), "side"),
        P(None, ("grp", "blk")),
        P(None, ("grp", "blk")),
        P(None, ("grp", "blk")),
        P(None, ("grp", "blk")),
        P(("grp", "blk"), None),
        P(("grp", "blk"), None),
        P(("grp", "blk"), None),
        P(("grp", "blk"), None),
        P(("grp", "blk"), None),
        P(("grp", "blk")),
        P(("grp", "blk")),
    )
    out_specs = (P(("grp", "blk"), "side"), P(("grp", "blk"), "side"))
    return jax.shard_map(body, mesh=mesh, in_specs=in_specs, out_specs=out_specs, check_vma=False)
```

profile of v0, /device:TPU:0, one launch (start us, length us, event | category | flops | bytes accessed | tf_op | source)
XLA Modules:
  0.0 343.9 jit_solution(12579196139999055338)
XLA Ops:
  7.2 1.0 slice_reduce_fusion.3
  8.3 9.2 %gather_fusion.1 = bf16[1536,3,128]{2,0,1:T(8,128)(2,1)S(1)} fusion(bf16[3,1024,128]{2,1,0:T(8,128)(2,1)} %param.18, s32[2048]{0:T(1024)S(1)} %pad_clamp_fusion.3), kind=kCustom, calls=%fused_computation.clone | custom fusion | bytes 2365440 | tf_op jit(solution)/shard_map/jit(_take)/gather | solution.py:53
  19.2 7.3 %gather_fusion.2 = bf16[1536,3,128]{2,0,1:T(8,128)(2,1)} fusion(bf16[3,1024,128]{2,1,0:T(8,128)(2,1)S(1)} %copy-done.1, s32[2048]{0:T(1024)S(1)} %pad_clamp_fusion.2), kind=kCustom, calls=%fused_computation.1.clone | custom fusion | bytes 2365440 | tf_op jit(solution)/shard_map/jit(_take)/gather | solution.py:53
  26.5 1.5 select_bitcast_fusion.2
  28.0 1.0 fusion.41
  29.1 7.3 %gather_fusion.3 = bf16[1536,3,128]{2,0,1:T(8,128)(2,1)} fusion(bf16[3,1024,128]{2,1,0:T(8,128)(2,1)S(1)} %copy-done.1, s32[2048]{0:T(1024)S(1)} %pad_clamp_fusion.1), kind=kCustom, calls=%fused_computation.2.clone | custom fusion | bytes 2365440 | tf_op jit(solution)/shard_map/jit(_take)/gather | solution.py:53
  36.4 1.5 select_bitcast_fusion.1
  37.9 1.1 fusion.42
  39.0 7.3 %gather_fusion.4 = bf16[1536,3,128]{2,0,1:T(8,128)(2,1)} fusion(bf16[3,1024,128]{2,1,0:T(8,128)(2,1)S(1)} %copy-done.1, s32[2048]{0:T(1024)S(1)} %pad_clamp_fusion), kind=kCustom, calls=%fused_computation.3.clone | custom fusion | bytes 2365440 | tf_op jit(solution)/shard_map/jit(_take)/gather | solution.py:53
  46.3 1.5 select_bitcast_fusion
  47.8 1.0 fusion.43
  50.1 6.0 %fusion.20 = bf16[4,4,96,128]{3,2,1,0:T(8,128)(2,1)} fusion(bf16[4,4,96,128]{3,2,1,0:T(8,128)(2,1)} %bitcast.101, bf16[4,4,96,128]{3,2,1,0:T(8,128)(2,1)} %bitcast.102, bf16[4,4,96,128]{3,2,1,0:T(8,128)(2,1)} %bitcast.100, bf16[4,4,96,128]{3,2,1,0:T(8,128)(2,1)} %bitcast.98, bf16[4,4,96,128]{3,2,1,0:T(8,128)(2,1)} %bitcast.99, ...), kind=kLoop, calls=%fused_computation.38 | loop fusion | flops 7077888 | bytes 5185536 | tf_op jit(solution)/shard_map/convert_element_type | solution.py:57
  56.1 5.2 %all-to-all-start = ((bf16[4,4,96,128]{3,2,1,0:T(8,128)(2,1)}), bf16[4,4,96,128]{3,2,1,0:T(8,128)(2,1)S(1)}, u32[]{:S(2)}, u32[]{:S(2)}) async-start(bf16[4,4,96,128]{3,2,1,0:T(8,128)(2,1)} %fusion.20), calls=%async_computation | async-start | bytes 786432 | tf_op jit(solution)/shard_map/all_to_all | solution.py:62
  63.8 43.5 %all-gather.2 = f32[512,32]{1,0:T(8,128)S(1)} all-gather(f32[32,32]{1,0:T(8,128)S(1)} %copy.70), channel_id=4, replica_groups=mesh['side'=2,'grp'=4,'blk'=4] {'grp','blk'}, dimensions={0}, use_global_device_ids=true | all-gather | bytes 69632 | tf_op jit(solution)/shard_map/all_gather | solution.py:11
  108.0 38.0 %all-gather = f32[512,32]{1,0:T(8,128)S(1)} all-gather(f32[32,32]{1,0:T(8,128)S(1)} %copy.68), channel_id=2, replica_groups=mesh['side'=2,'grp'=4,'blk'=4] {'grp','blk'}, dimensions={0}, use_global_device_ids=true | all-gather | bytes 69632 | tf_op jit(solution)/shard_map/all_gather | solution.py:11
  146.8 3.5 %all-to-all-start.1 = ((bf16[4,4,96,128]{3,2,0,1:T(8,128)(2,1)}), bf16[4,4,96,128]{3,2,0,1:T(8,128)(2,1)S(1)}, u32[]{:S(2)}, u32[]{:S(2)}) async-start(bf16[4,4,96,128]{3,2,0,1:T(8,128)(2,1)} %copy.66), calls=%async_computation.1 | async-start | bytes 786432 | tf_op jit(solution)/shard_map/all_to_all | solution.py:61
  150.3 8.7 %all-to-all-done.1 = bf16[4,4,96,128]{3,2,0,1:T(8,128)(2,1)S(1)} async-done(((bf16[4,4,96,128]{3,2,0,1:T(8,128)(2,1)}), bf16[4,4,96,128]{3,2,0,1:T(8,128)(2,1)S(1)}, u32[]{:S(2)}, u32[]{:S(2)}) %all-to-all-start.1) | async-done | bytes 393248 | tf_op jit(solution)/shard_map/all_to_all | solution.py:61
  159.1 3.2 gather_fusion
  163.4 2.3 all_gather.35
  166.1 38.7 %all-gather.1 = f32[512,128]{1,0:T(8,128)S(1)} all-gather(f32[32,128]{1,0:T(8,128)S(1)} %convolution_bitcast_fusion.3), channel_id=3, replica_groups=mesh['side'=2,'grp'=4,'blk'=4] {'grp','blk'}, dimensions={0}, use_global_device_ids=true | all-gather | bytes 278528 | tf_op jit(solution)/shard_map/all_gather | solution.py:11
  204.8 2.7 while.28
  208.6 39.0 %all-gather.3 = f32[512,128]{1,0:T(8,128)S(1)} all-gather(f32[32,128]{1,0:T(8,128)S(1)} %convolution_bitcast_fusion.2), channel_id=5, replica_groups=mesh['side'=2,'grp'=4,'blk'=4] {'grp','blk'}, dimensions={0}, use_global_device_ids=true | all-gather | bytes 278528 | tf_op jit(solution)/shard_map/all_gather | solution.py:11
  248.3 13.8 %while.29 = (s32[]{:T(128)}, f32[32,128]{1,0:T(8,128)S(1)}, s32[]{:T(128)}, f32[16,32,32]{2,1,0:T(8,128)}, f32[16,32,128]{2,1,0:T(8,128)}, /*index=5*/s32[]{:T(128)}, s32[]{:T(128)}) while((s32[]{:T(128)}, f32[32,128]{1,0:T(8,128)S(1)}, s32[]{:T(128)}, f32[16,32,32]{2,1,0:T(8,128)}, f32[16,32,128]{2,1,0:T(8,128)}, ...), condition=%wide.region_6.8_spmd.clone, body=%wide.region_5.7_spmd.clone.sunk | while | flops 1589252 | bytes 117343 | solution.py:23
  264.4 72.6 %reduce-scatter.2.cloned.1.call-done = f32[16,128]{1,0:T(8,128)} async-done(((f32[256,128]{1,0:T(8,128)}), f32[16,128]{1,0:T(8,128)}) %reduce-scatter.2.cloned.1.call-update) | async-done | bytes 8208 | tf_op jit(solution)/shard_map/reduce_scatter | solution.py:103
  (150 shorter events, 27.1 us)
Async XLA Ops:
  7.2 55.1 %copy-start = (bf16[1024,1024]{1,0:T(8,128)(2,1)S(1)}, bf16[1024,1024]{1,0:T(8,128)(2,1)}, u32[]{:S(2)}) copy-start(bf16[1024,1024]{1,0:T(8,128)(2,1)} %param.23) | copy-start | bytes 6291460
  17.8 1.4 copy-start.1
  47.8 1.1 copy-start.11
  47.8 1.1 copy-start.12
  47.8 2.2 copy-start.3
  47.8 2.2 copy-start.4
  50.0 11.2 %copy-start.16 = (s32[16,1]{0,1:T(1,128)S(1)}, s32[16,1]{0,1:T(1,128)}, u32[]{:S(2)}) copy-start(s32[16,1]{0,1:T(1,128)} %param.22) | copy-start | bytes 196
  50.1 12.3 %copy-start.6 = (bf16[1024,32]{0,1:T(8,128)(2,1)S(1)}, bf16[1024,32]{0,1:T(8,128)(2,1)}, u32[]{:S(2)}) copy-start(bf16[1024,32]{0,1:T(8,128)(2,1)} %param.24) | copy-start | bytes 196612
  56.1 89.9 %all-to-all-start = ((bf16[4,4,96,128]{3,2,1,0:T(8,128)(2,1)}), bf16[4,4,96,128]{3,2,1,0:T(8,128)(2,1)S(1)}, u32[]{:S(2)}, u32[]{:S(2)}) async-start(bf16[4,4,96,128]{3,2,1,0:T(8,128)(2,1)} %fusion.20), calls=%async_computation | async-start | bytes 786432 | tf_op jit(solution)/shard_map/all_to_all | solution.py:62
  61.3 1.8 copy-start.5
  61.6 84.4 %copy-start.9 = (s32[1024]{0:T(1024)}, s32[1024]{0:T(1024)S(1)}, u32[]{:S(2)}) copy-start(s32[1024]{0:T(1024)S(1)} %convert_reduce_fusion) | copy-start | bytes 12292
  62.3 1.0 copy-start.14
  62.3 1.0 copy-start.7
  62.3 1.0 copy-start.8
  146.0 4.3 %copy-start.10 = (s32[1024]{0:T(1024)S(1)}, s32[1024]{0:T(1024)}, u32[]{:S(2)}) copy-start(s32[1024]{0:T(1024)} %copy-done.9) | copy-start | bytes 12292
  146.8 12.3 %all-to-all-start.1 = ((bf16[4,4,96,128]{3,2,0,1:T(8,128)(2,1)}), bf16[4,4,96,128]{3,2,0,1:T(8,128)(2,1)S(1)}, u32[]{:S(2)}, u32[]{:S(2)}) async-start(bf16[4,4,96,128]{3,2,0,1:T(8,128)(2,1)} %copy.66), calls=%async_computation.1 | async-start | bytes 786432 | tf_op jit(solution)/shard_map/all_to_all | solution.py:61
  150.2 186.8 %reduce-scatter.2.cloned.1.call-start = ((), (), s32[]{:S(2)}) async-start(), calls=%async_computation.3 | async-start | bytes 139264 | tf_op jit(solution)/shard_map/reduce_scatter | solution.py:103
  208.6 53.5 %copy-start.15 = (pred[32]{0:T(512)(128)(4,1)S(1)}, pred[32]{0:T(512)(128)(4,1)}, u32[]{:S(2)}) copy-start(pred[32]{0:T(512)(128)(4,1)} %copy-done.14) | copy-start | bytes 100
  208.6 54.0 %copy-start.2 = (bf16[1024,256]{1,0:T(8,128)(2,1)S(1)}, bf16[1024,256]{1,0:T(8,128)(2,1)}, u32[]{:S(2)}) copy-start(bf16[1024,256]{1,0:T(8,128)(2,1)} %all_gather.35) | copy-start | bytes 1572868
  208.6 54.0 %copy-start.13 = (f32[1024]{0:T(1024)S(1)}, f32[1024]{0:T(1024)}, u32[]{:S(2)}) copy-start(f32[1024]{0:T(1024)} %param.29) | copy-start | bytes 12292
Sparse Core Ops, SparseCore 0:
  263.7 73.2 reduce-scatter.1
where the time goes:
time: 347 us; the launch traced here: 344 us
  blocking collectives  161 us (46%)
  waiting for transfers between devices  81.4 us (23%)
  local copies, waits for them, and re-layouts  44.3 us (13%)
  matrix products  20.1 us (6%)
  between operations  15.1 us (4%)
  other arithmetic  11.8 us (3%)
  starting transfers between devices  8.66 us (2%)
    all_gather x4, blocking collectives, entering(): pieces = jax.tree.map(lambda part: lax.all_gather(part, axis), value)  159 us
    reduce_scatter x1, waiting for transfers between devices, body(): lax.psum_scatter(lax.dot_general(all_modes, weighted, (((0,), (0,)), ((),...  72.6 us
    gather x4, local copies, waits for them, and re-layouts, body(): picked = jnp.take(node_modes, node_index[corner], axis=1)  31.1 us
    dot_general x30, matrix products, compose(): jnp.dot(later[0], earlier[1], precision=HIGH) + later[1]  15.4 us
    all_to_all x1, waiting for transfers between devices, body(): lax.all_to_all(lax.all_to_all(sectioned, 'grp', split_axis=0, concat_axis...  8.74 us
  transfers between devices with their start and end apart: 3, of which 2 were waited for; matrix products, arithmetic and copies ran while one was open for 1% of the time, Pallas kernels for 0%

commit v1 on v0

v1 whole, which is shorter than its diff:
```python
import functools

import jax
import jax.numpy as jnp
from jax import lax
from jax.experimental import pallas as pl
from jax.experimental.pallas import tpu as pltpu
from jax.sharding import PartitionSpec as P

MESH = pl.DeviceIdType.MESH
F32 = jnp.float32
BF16 = jnp.bfloat16
TILE = 16


def dot(a, b):
    return jnp.dot(a, b, preferred_element_type=F32)


def dot_rows(a, b):
    return lax.dot_general(a, b, (((0,), (0,)), ((), ())), preferred_element_type=F32)


def split(a):
    high = a.astype(BF16)
    return high, (a - high.astype(F32)).astype(BF16)


def kernel(
    ng,
    nb,
    cap,
    out_rows,
    modes_hbm,
    index_hbm,
    interp_hbm,
    normals_hbm,
    counts,
    diag_hbm,
    ll_hbm,
    lr_hbm,
    ul_hbm,
    ur_hbm,
    ranks,
    areas_hbm,
    pot_hbm,
    mass_ref,
    modes,
    index,
    interp,
    normals,
    diag,
    ll,
    lr,
    ul,
    ur,
    areas,
    rows_pack,
    cols,
    wbuf,
    sendbuf,
    arrived,
    pick,
    maps,
    back_terms,
    kout,
    wcat,
    gp,
    solved,
    velocities,
    velocities_t,
    zall,
    psend,
    precv,
    pot,
    msend,
    mrecv,
    local_sem,
    map_send,
    map_recv,
    slab_send,
    slab_recv,
    vel_send,
    vel_recv,
    side_send,
    side_recv,
    z_send,
    z_recv,
    p_send,
    p_recv,
    m_send,
    m_recv,
):
    nd = ng * nb
    rank_width = ll.shape[1]
    two = 2 * rank_width
    panels = diag.shape[0]
    nodes, width3 = modes.shape
    width = width3 // 3
    slots = nd * cap
    side, my_g, my_b = lax.axis_index("side"), lax.axis_index("grp"), lax.axis_index("blk")
    me = my_g * nb + my_b

    barrier = pltpu.get_barrier_semaphore()

    @pl.loop(1, nd)
    def _(k):
        other = lax.rem(me + k, nd)
        pl.semaphore_signal(
            barrier, inc=1, device_id=(side, other // nb, lax.rem(other, nb)), device_id_type=MESH
        )

    pl.semaphore_signal(barrier, inc=1, device_id=(1 - side, my_g, my_b), device_id_type=MESH)

    pairs = [
        (diag_hbm, diag),
        (lr_hbm, lr),
        (ur_hbm, ur),
        (ll_hbm, ll),
        (ul_hbm, ul),
        (index_hbm, index),
        (interp_hbm, interp),
        (normals_hbm, normals),
        (areas_hbm, areas),
    ] + [(modes_hbm.at[c], modes.at[:, c * width : (c + 1) * width]) for c in range(3)]
    loads = [pltpu.make_async_copy(a, b, local_sem.at[i]) for i, (a, b) in enumerate(pairs)]
    for load in (loads[5], loads[6], loads[7], *loads[0:5], *loads[9:12], loads[8]):
        load.start()

    for i in (5, 6, 7):
        loads[i].wait()
    rows_pack[...] = jnp.zeros_like(rows_pack)
    rows_pack[0:4, :] = index[...].astype(F32)
    rows_pack[4:8, :] = interp[...]
    rows_pack[8:11, :] = normals[...]
    cols[...] = rows_pack[...].T

    for i in range(5):
        loads[i].wait()
    keep = lax.broadcasted_iota(jnp.int32, (panels, rank_width), 1) < ranks[0]
    lower = jnp.where(keep, ll[...].astype(F32), 0.0).astype(BF16)
    upper = jnp.where(keep, ul[...].astype(F32), 0.0).astype(BF16)
    right = jnp.concatenate([lr[...], ur[...]], axis=1)
    w_high, w_low = split(dot_rows(right, diag[...]))
    wcat[0:two, :] = w_high
    wcat[two : 2 * two, :] = w_low
    both = dot(wcat[...], lower)
    both = both[0:two] + both[two : 2 * two]
    top = dot_rows(ur[...], upper)
    maps[me] = jnp.concatenate(
        [both[0:rank_width], both[rank_width:two], top, jnp.zeros_like(top)], axis=1
    )

    pl.semaphore_wait(barrier, nd)

    def map_copy(k, b):
        return pltpu.make_async_remote_copy(
            src_ref=maps.at[me],
            dst_ref=maps.at[me],
            send_sem=map_send.at[k],
            recv_sem=map_recv.at[k],
            device_id=(side, my_g, b),
            device_id_type=MESH,
        )

    @pl.loop(1, nb)
    def _(k):
        map_copy(k, lax.rem(my_b + k, nb)).start()

    for i in (9, 10, 11):
        loads[i].wait()

    def slab_copy(k, g):
        return pltpu.make_async_remote_copy(
            src_ref=maps.at[pl.ds(my_g * nb, nb)],
            dst_ref=maps.at[pl.ds(my_g * nb, nb)],
            send_sem=slab_send.at[k],
            recv_sem=slab_recv.at[k],
            device_id=(side, g, my_b),
            device_id_type=MESH,
        )

    def vel_copy(kg, kb, g, b):
        return pltpu.make_async_remote_copy(
            src_ref=sendbuf.at[g * nb + b],
            dst_ref=arrived.at[me],
            send_sem=vel_send.at[kg, kb],
            recv_sem=vel_recv.at[kg, kb],
            device_id=(side, g, b),
            device_id_type=MESH,
        )

    chunk = nb * cap
    node_ids = lax.broadcasted_iota(jnp.int32, (TILE, nodes), 1).astype(F32)

    def velocity_chunk(g):
        base = g * chunk

        @pl.loop(0, chunk // TILE, unroll=2)
        def _(i):
            mine = cols[pl.ds(pl.multiple_of(base + i * TILE, TILE), TILE), :]
            total = jnp.zeros((TILE, nodes), F32)
            for k in range(4):
                total += jnp.where(node_ids == mine[:, k : k + 1], mine[:, 4 + k : 5 + k], 0.0)
            wbuf[pl.ds(pl.multiple_of(i * TILE, TILE), TILE), :] = total.astype(BF16)

        moved = dot(wbuf[...], modes[...])
        normal = cols[pl.ds(pl.multiple_of(base, TILE), chunk), :]
        velocity = normal[:, 8:9] * moved[:, 0:width]
        for c in (1, 2):
            velocity += normal[:, 8 + c : 9 + c] * moved[:, c * width : (c + 1) * width]
        sendbuf[pl.ds(g * nb, nb)] = velocity.astype(BF16).reshape(nb, cap, width)

    def velocity_send(kg, g):
        @pl.loop(jnp.where(kg == 0, 1, 0), nb)
        def _(k):
            vel_copy(kg, k, g, lax.rem(my_b + k, nb)).start()

    first = lax.rem(my_g + 1, ng)
    velocity_chunk(first)

    @pl.loop(1, nb)
    def _(k):
        map_copy(k, lax.rem(my_b + k, nb)).wait()

    @pl.loop(1, ng)
    def _(k):
        slab_copy(k, lax.rem(my_g + k, ng)).start()

    velocity_send(lax.rem(jnp.int32(1), ng), first)

    @pl.loop(1, ng)
    def _(step):
        kg = lax.rem(step + 1, ng)
        g = lax.rem(my_g + kg, ng)
        velocity_chunk(g)
        velocity_send(kg, g)

    arrived[me] = sendbuf[me]

    slot_ids = lax.broadcasted_iota(jnp.int32, (1, slots), 1)

    def place(j, carry):
        offset, target = carry
        local = slot_ids - j * cap
        count = counts[j, 0]
        target = jnp.where((local >= 0) & (local < count), local + offset, target)
        return offset + count, target

    _, target = lax.fori_loop(
        0, nd, place, (jnp.int32(0), jnp.full((1, slots), -1, jnp.int32))
    )
    panel_ids = lax.broadcasted_iota(jnp.int32, (TILE, slots), 0)

    @pl.loop(0, panels // TILE, unroll=2)
    def _(i):
        hot = jnp.where(panel_ids + i * TILE == target, 1.0, 0.0)
        pick[pl.ds(pl.multiple_of(i * TILE, TILE), TILE), :] = hot.astype(BF16)

    g_high, g_low = split(dot(diag[...], lower))
    gp[...] = jnp.concatenate([g_high, g_low, g_high, upper, upper], axis=1)

    @pl.loop(1, ng)
    def _(k):
        slab_copy(k, lax.rem(my_g + k, ng)).wait()

    units = ng * two
    row_id = lax.broadcasted_iota(jnp.int32, (rank_width, units), 0)
    col_id = lax.broadcasted_iota(jnp.int32, (rank_width, units), 1)

    def impulse(i, shift):
        gi, bi = i // nb, lax.rem(i, nb)
        hit = jnp.where(bi == my_b, 1.0, 0.0).astype(F32)
        return jnp.where(col_id == row_id + (two * gi + shift), hit, 0.0)

    def three(high, low):
        return jnp.concatenate([high, low, high], axis=1)

    def state(s):
        high, low = split(s)
        return jnp.concatenate([high, high, low], axis=0)

    def forward(i, s):
        high, low = split(maps[i])
        lhs = jnp.concatenate(
            [
                three(high[:, 0:rank_width], low[:, 0:rank_width]),
                three(high[:, rank_width:two], low[:, rank_width:two]),
            ],
            axis=0,
        )

        @pl.when(i // nb == my_g)
        def _():
            kout[lax.rem(i, nb), 0:rank_width, :] = s

        moved = dot(lhs, state(s))
        back_terms[i] = moved[rank_width:two]
        return s - moved[0:rank_width] + impulse(i, 0)

    def backward(step, t):
        i = nd - 1 - step
        high, low = split(maps[i])
        lhs = three(high[:, two : two + rank_width], low[:, two : two + rank_width])

        @pl.when(i // nb == my_g)
        def _():
            kout[lax.rem(i, nb), rank_width:two, :] = t

        return t - dot(lhs, state(t)) + impulse(i, rank_width) - back_terms[i]

    zero = jnp.zeros((rank_width, units), F32)
    lax.fori_loop(0, nd, forward, zero)
    lax.fori_loop(0, nd, backward, zero)

    loads[8].wait()
    area = areas[...].T

    @pl.loop(0, nd - 1)
    def _(k):
        source = k + 1
        vel_copy(source // nb, lax.rem(source, nb), my_g, my_b).wait_recv()

    b = dot(pick[...], arrived[...].reshape(slots, width)).astype(BF16)
    velocities[side] = b
    side_copy = pltpu.make_async_remote_copy(
        src_ref=velocities.at[side],
        dst_ref=velocities.at[side],
        send_sem=side_send,
        recv_sem=side_recv,
        device_id=(1 - side, my_g, my_b),
        device_id_type=MESH,
    )
    z = dot(wcat[...], b)
    zall[my_g] = (z[0:two] + z[two : 2 * two]).astype(BF16)

    def z_copy(k, g):
        return pltpu.make_async_remote_copy(
            src_ref=zall.at[my_g],
            dst_ref=zall.at[my_g],
            send_sem=z_send.at[k],
            recv_sem=z_recv.at[k],
            device_id=(side, g, my_b),
            device_id_type=MESH,
        )

    @pl.loop(1, ng)
    def _(k):
        z_copy(k, lax.rem(my_g + k, ng)).start()

    side_copy.start()
    solved[...] = dot(diag[...], b)

    @pl.loop(1, ng)
    def _(k):
        z_copy(k, lax.rem(my_g + k, ng)).wait()

    k_high, k_low = split(kout[...].reshape(nb * two, units))
    zcat = zall[...].reshape(units, width)
    part = dot(k_high, zcat) + dot(k_low, zcat)
    psend[...] = part.astype(BF16).reshape(nb, two, width)

    def p_copy(k, b):
        return pltpu.make_async_remote_copy(
            src_ref=psend.at[b],
            dst_ref=precv.at[my_b],
            send_sem=p_send.at[k],
            recv_sem=p_recv.at[k],
            device_id=(side, my_g, b),
            device_id_type=MESH,
        )

    @pl.loop(1, nb)
    def _(k):
        p_copy(k, lax.rem(my_b + k, nb)).start()

    precv[my_b] = psend[my_b]
    side_copy.wait()
    for h in range(2):
        velocities_t[h * width : (h + 1) * width, :] = velocities[h].T

    @pl.loop(1, nb)
    def _(k):
        p_copy(k, lax.rem(my_b + k, nb)).wait()

    states = jnp.sum(precv[...].astype(F32), axis=0)
    s_high, s_low = split(states[0:rank_width])
    t_high, t_low = split(states[rank_width:two])
    rhs = jnp.concatenate([s_high, s_high, s_low, t_high, t_low], axis=0)
    potentials = (solved[...] - dot(gp[...], rhs)).astype(BF16)
    pot[...] = potentials
    pot_copy = pltpu.make_async_copy(pot, pot_hbm, local_sem.at[len(pairs)])
    pot_copy.start()
    weighted = (area[:, 0:1] * potentials.astype(F32)).astype(BF16)
    partial = dot(velocities_t[...], weighted).astype(BF16)
    held = msend.shape[1]
    if held != out_rows:
        row = lax.broadcasted_iota(jnp.int32, (nd * held, nd * out_rows), 0)
        col = lax.broadcasted_iota(jnp.int32, (nd * held, nd * out_rows), 1)
        home = (col // out_rows) * held + col % out_rows
        partial = dot(jnp.where(row == home, 1.0, 0.0).astype(BF16), partial).astype(BF16)
    msend[...] = partial.reshape(nd, held, width)

    def m_copy(k, d):
        return pltpu.make_async_remote_copy(
            src_ref=msend.at[d],
            dst_ref=mrecv.at[me],
            send_sem=m_send.at[k],
            recv_sem=m_recv.at[k],
            device_id=(side, d // nb, lax.rem(d, nb)),
            device_id_type=MESH,
        )

    @pl.loop(1, nd)
    def _(k):
        m_copy(k, lax.rem(me + k, nd)).start()

    mrecv[me] = msend[me]

    @pl.loop(0, nd - 1)
    def _(k):
        source = k + 1
        vel_copy(source // nb, lax.rem(source, nb), my_g, my_b).wait_send()

    @pl.loop(1, nd)
    def _(k):
        m_copy(k, lax.rem(me + k, nd)).wait()

    mass_ref[...] = jnp.sum(mrecv[...].astype(F32), axis=0)[0:out_rows]
    pot_copy.wait()


def body(
    node_modes,
    node_index,
    interp,
    normals,
    counts,
    inverse_diag,
    lower_left,
    lower_right,
    upper_left,
    upper_right,
    ranks,
    areas,
):
    ng, nb = lax.axis_size("grp"), lax.axis_size("blk")
    nd = ng * nb
    nodes, width = node_modes.shape[1:]
    cap_given = node_index.shape[1] // nd
    cap = -(-cap_given // TILE) * TILE
    if cap != cap_given:

        def widen(part):
            lead = part.shape[0]
            spare = ((0, 0), (0, 0), (0, cap - cap_given))
            return jnp.pad(part.reshape(lead, nd, cap_given), spare).reshape(lead, nd * cap)

        node_index, interp, normals = widen(node_index), widen(interp), widen(normals)
    slots = nd * cap
    panels = inverse_diag.shape[0]
    rank_width = lower_left.shape[1]
    two = 2 * rank_width
    units = ng * two
    out_rows = 2 * width // nd
    held = -(-out_rows // TILE) * TILE
    areas = areas.reshape(1, panels)
    hbm = pl.BlockSpec(memory_space=pl.ANY)
    smem = pl.BlockSpec(memory_space=pltpu.SMEM)
    vmem = pl.BlockSpec(memory_space=pltpu.VMEM)
    dma = pltpu.SemaphoreType.DMA
    factor = pltpu.VMEM((panels, rank_width), BF16)
    scratch = [
        pltpu.VMEM((nodes, 3 * width), BF16),
        pltpu.VMEM((4, slots), jnp.int32),
        pltpu.VMEM((4, slots), F32),
        pltpu.VMEM((3, slots), F32),
        pltpu.VMEM((panels, panels), BF16),
        factor,
        factor,
        factor,
        factor,
        pltpu.VMEM((1, panels), F32),
        pltpu.VMEM((TILE, slots), F32),
        pltpu.VMEM((slots, TILE), F32),
        pltpu.VMEM((nb * cap, nodes), BF16),
        pltpu.VMEM((nd, cap, width), BF16),
        pltpu.VMEM((nd, cap, width), BF16),
        pltpu.VMEM((panels, slots), BF16),
        pltpu.VMEM((nd, rank_width, 4 * rank_width), F32),
        pltpu.VMEM((nd, rank_width, units), F32),
        pltpu.VMEM((nb, two, units), F32),
        pltpu.VMEM((2 * two, panels), BF16),
        pltpu.VMEM((panels, 5 * rank_width), BF16),
        pltpu.VMEM((panels, width), F32),
        pltpu.VMEM((2, panels, width), BF16),
        pltpu.VMEM((2 * width, panels), BF16),
        pltpu.VMEM((ng, two, width), BF16),
        pltpu.VMEM((nb, two, width), BF16),
        pltpu.VMEM((nb, two, width), BF16),
        pltpu.VMEM((panels, width), BF16),
        pltpu.VMEM((nd, held, width), BF16),
        pltpu.VMEM((nd, held, width), BF16),
        dma((13,)),
        dma((nb,)),
        dma((nb,)),
        dma((ng,)),
        dma((ng,)),
        dma((ng, nb)),
        dma((ng, nb)),
        dma(()),
        dma(()),
        dma((ng,)),
        dma((ng,)),
        dma((nb,)),
        dma((nb,)),
        dma((nd,)),
        dma((nd,)),
    ]
    return pl.pallas_call(
        functools.partial(kernel, ng, nb, cap, out_rows),
        out_shape=(
            jax.ShapeDtypeStruct((panels, width), BF16),
            jax.ShapeDtypeStruct((out_rows, width), F32),
        ),
        in_specs=[hbm, hbm, hbm, hbm, smem, hbm, hbm, hbm, hbm, hbm, smem, hbm],
        out_specs=(hbm, vmem),
        scratch_shapes=scratch,
        compiler_params=pltpu.CompilerParams(
            collective_id=0, has_side_effects=True, vmem_limit_bytes=56 * 1024 * 1024
        ),
    )(
        node_modes,
        node_index,
        interp,
        normals,
        counts,
        inverse_diag,
        lower_left,
        lower_right,
        upper_left,
        upper_right,
        ranks,
        areas,
    )


def solution(mesh):
    split_rows = P(("grp", "blk"), None)
    split_cols = P(None, ("grp", "blk"))
    in_specs = (
        P(None, ("grp", "blk"), "side"),
        split_cols,
        split_cols,
        split_cols,
        split_cols,
        split_rows,
        split_rows,
        split_rows,
        split_rows,
        split_rows,
        P(("grp", "blk")),
        P(("grp", "blk")),
    )
    out_specs = (P(("grp", "blk"), "side"), P(("grp", "blk"), "side"))
    return jax.shard_map(body, mesh=mesh, in_specs=in_specs, out_specs=out_specs, check_vma=False)
```

time: 347 us -> 55.4 us (0.16)
  blocking collectives: 161 us -> 0 us
  waiting for transfers between devices: 81.4 us -> 0 us
  Pallas kernels: 0 us -> 42.7 us
  local copies, waits for them, and re-layouts: 44.3 us -> 11 us
  matrix products: 20.1 us -> 0 us
  between operations: 15.1 us -> 1.29 us
  other arithmetic: 11.8 us -> 0 us
  starting transfers between devices: 8.66 us -> 0 us
    all_gather x5 -> x0, blocking collectives: 161 us -> none  [the longest x4 159 us: entering(): pieces = jax.tree.map(lambda part: lax.all_gather(part, axis), value)]
    reduce_scatter x1 -> x0, waiting for transfers between devices: 72.6 us -> none  [body(): lax.psum_scatter(lax.dot_general(all_modes, weighted, (((0,), (0,)), ((),...]
    pallas_call x0 -> x1, Pallas kernels: none -> 42.7 us  [body(): pl.pallas_call(functools.partial(kernel, ng, nb, cap, out_rows), out_shap...]
    gather x5 -> x0, local copies, waits for them, and re-layouts: 34.3 us -> none  [the longest x4 31.1 us: body(): picked = jnp.take(node_modes, node_index[corner], axis=1)]
    dot_general x39 -> x0, matrix products: 20.1 us -> none  [the longest x30 15.4 us: compose(): jnp.dot(later[0], earlier[1], precision=HIGH) + later[1]]
    unnamed x36 -> x7, local copies, waits for them, and re-layouts: 1.5 us -> 11 us
    all_to_all x2 -> x0, waiting for transfers between devices: 8.74 us -> none  [the longest x1 8.74 us: body(): lax.all_to_all(lax.all_to_all(sectioned, 'grp', split_axis=0, concat_axis...]
    all_to_all x2 -> x0, starting transfers between devices: 8.62 us -> none  [the longest x1 5.16 us: body(): lax.all_to_all(sectioned, 'grp', split_axis=0, concat_axis=0, tiled=True)]
  transfers between devices with their start and end apart: 3 -> 0, of which waited for: 2 -> 0; matrix products, arithmetic and copies ran while one was open for 1% -> 0% of each run, Pallas kernels for 0% -> 0%
where the time goes in v1:
time: 55.4 us; the launch traced here: 55 us
  Pallas kernels  42.7 us (77%)
  local copies, waits for them, and re-layouts  11 us (20%)
  between operations  1.29 us (2%)
    pallas_call x1, Pallas kernels, body(): pl.pallas_call(functools.partial(kernel, ng, nb, cap, out_rows), out_shap...  42.7 us
    unnamed x7, local copies, waits for them, and re-layouts  11 us

profile of v1, /device:TPU:0, one launch (start us, length us, event | category | flops | bytes accessed | tf_op | source)
XLA Modules:
  0.0 55.0 jit_solution(4623182886580075194)
XLA Ops:
  1.3 1.3 %copy.14.counts = s32[16,1]{1,0:T(8,128)} copy(s32[16,1]{0,1:T(1,128)} %param.16) | data formatting | bytes 128 | tf_op args[4]
  2.6 1.7 %copy.15.ll_hbm = bf16[1024,32]{1,0:T(8,128)(2,1)} copy(bf16[1024,32]{0,1:T(8,128)(2,1)} %param.18) | data formatting | bytes 131072 | tf_op args[6]
  4.3 1.7 %copy.16.lr_hbm = bf16[1024,32]{1,0:T(8,128)(2,1)} copy(bf16[1024,32]{0,1:T(8,128)(2,1)} %param.19) | data formatting | bytes 131072 | tf_op args[7]
  6.0 1.7 %copy.17.ul_hbm = bf16[1024,32]{1,0:T(8,128)(2,1)} copy(bf16[1024,32]{0,1:T(8,128)(2,1)} %param.20) | data formatting | bytes 131072 | tf_op args[8]
  7.6 1.7 %copy.18.ur_hbm = bf16[1024,32]{1,0:T(8,128)(2,1)} copy(bf16[1024,32]{0,1:T(8,128)(2,1)} %param.21) | data formatting | bytes 131072 | tf_op args[9]
  9.3 42.7 %shard_map.131 = (bf16[1024,128]{1,0:T(8,128)(2,1)}, f32[16,128]{1,0:T(8,128)}) custom-call(bf16[3,1024,128]{2,1,0:T(8,128)(2,1)} %modes_hbm.1, s32[4,1536]{1,0:T(4,128)} %index_hbm.1, f32[4,1536]{1,0:T(4,128)} %interp_hbm.1, f32[3,1536]{1,0:T(4,128)} %normals_hbm.1, s32[16,1]{1,0:T(8,128)} %copy.14.counts, bf16[1024,1024]{1,0:T(8,128)(2,1)} %diag_hbm.1, ...), custom_call_target="tpu_custom_call" | custom-call | tf_op jit(solution)/shard_map/pallas_call | solution.py:520
  52.0 1.7 %copy.22 = bf16[1024,128]{1,0:T(8,128)(2,1)} copy(bf16[1024,128]{1,0:T(8,128)(2,1)} %get-tuple-element.4) | data formatting | bytes 524288
  53.7 1.3 %copy.23 = f32[16,128]{1,0:T(8,128)} copy(f32[16,128]{1,0:T(8,128)} %get-tuple-element.5) | data formatting | bytes 16384
